TPU v7x, 32 devices: a whole 2x2x4 slice. The times are simulated.
32 devices in a mesh: rows: 8 (over y, x, core), upd: 4 (over z).
Axes of the slice: x: 2, y: 2, z: 4, core: 2. Of those that a mesh axis runs over, the one named last changes fastest.
Arguments:
- tile_factors: bfloat16 [8, 32, 1024, 128], P('rows', 'upd'), may hold values from -6 to 6
- panel_factors: bfloat16 [32, 1024, 128], P('upd', 'rows'), may hold values from -0.1875 to 0.1875
- nonnull: int32 [8, 32], P('rows', 'upd'), may hold values from 0 to 1, as said below
- sketch: float32 [64, 1024], replicated, may hold values from -6 to 6
Outputs:
- update_factors: float32 [8, 1024, 128], P('rows', 'upd')
Inputs may be any that keep to these rules, and one draw needn't show every extreme that they name: In every aligned block of 8 update indices the first one is nonnull for every tile row.
All inputs are finite; a program needn't handle non-finite values.
Results may differ from a plain program's by a relative error of at most 0.0003.
Values may be sent and summed in bfloat16 or wider, within the bound.
A program may use at most 64 MiB of HBM per device.

v0:
```python
import jax
import jax.numpy as jnp
from jax import lax
from jax.sharding import PartitionSpec as P


def from_partner(shard, axis, stride):
    return lax.ppermute(shard, axis, [(i, i ^ 1 << stride) for i in range(lax.axis_size(axis))])


def compress(lefts, rights, sketch):
    hi = lax.Precision.HIGHEST
    proj = jnp.einsum("nbr,sb->nrs", rights, sketch, precision=hi)
    span = jnp.einsum("nbr,nrs->bs", lefts, proj, precision=hi)
    gram = jnp.dot(span.T, span, precision=hi)
    order = gram.shape[0]
    shift = 0.001 * jnp.trace(gram) / order + 1e-20
    gram = gram + shift * jnp.eye(order, dtype=gram.dtype)
    chol = jnp.linalg.cholesky(gram)
    basis = lax.linalg.triangular_solve(chol, span, left_side=False, lower=True, transpose_a=True)
    coef = jnp.einsum("nbr,bs->nrs", lefts, basis, precision=hi)
    image = jnp.einsum("nbr,nrs->bs", rights, coef, precision=hi)
    return (basis, image)


def merge_pair(pair, sketch, rank):
    basis, image = compress(pair[:, :, :rank], pair[:, :, rank:], sketch)
    return jnp.concatenate([basis, image], axis=-1)


def body(tile_factors, panel_factors, nonnull, sketch):
    rank = tile_factors.shape[3] // 2
    tiles = tile_factors[0]
    own_right = tiles[:, :, rank:]
    panel = lax.all_gather(panel_factors, "rows", axis=1, tiled=True)
    inner = jnp.einsum(
        "kbr,kbs->krs", own_right, panel[:, :, rank:], preferred_element_type=jnp.float32
    )
    far_left = panel[:, :, :rank]
    weight = nonnull[0].astype(jnp.float32)
    lefts = jnp.einsum(
        "kbr,krs->kbs",
        tiles[:, :, :rank].astype(jnp.float32),
        inner,
        precision=lax.Precision.HIGHEST,
    )
    lefts = lefts * weight[:, None, None]
    basis, image = compress(lefts, far_left.astype(jnp.float32), sketch)
    packed = jnp.concatenate([basis, image], axis=-1)
    levels = lax.axis_size("upd").bit_length() - 1
    for level in range(levels):
        other = from_partner(packed, "upd", level)
        upper = lax.axis_index("upd") >> level & 1 == 1
        low = jnp.where(upper, other, packed)
        high = jnp.where(upper, packed, other)
        packed = merge_pair(jnp.stack([low, high]), sketch, rank)
    scale = jnp.float32(packed.shape[0]) ** 0.5
    result = jnp.concatenate([packed[:, :rank] * scale, packed[:, rank:] / scale], axis=-1)
    share = packed.shape[0] // lax.axis_size("upd")
    mine = lax.dynamic_slice_in_dim(result, lax.axis_index("upd") * share, share, 0)
    return mine[None]


def solution(mesh):
    in_specs = (P("rows", "upd", None, None), P("upd", "rows", None), P("rows", "upd"), P())
    out_specs = P("rows", "upd", None)
    return jax.shard_map(body, mesh=mesh, in_specs=in_specs, out_specs=out_specs, check_vma=False)
```

profile of v0, /device:TPU:0, one launch (start us, length us, event | category | flops | bytes accessed | tf_op | source)
XLA Modules:
  0.0 147.3 jit_solution(15993294017863616955)
XLA Ops:
  6.5 1.8 %copy.17 = bf16[8,128,128]{1,2,0:T(8,128)(2,1)} copy(bf16[8,128,128]{2,1,0:T(8,128)(2,1)} %param.8) | data formatting | bytes 524288 | tf_op args[1]
  8.4 0.0 all-gather.2.cloned.1.call-update
  8.4 0.0 copy-start.4
  8.4 2.9 %copy.16 = bf16[1,8,1024,128]{2,3,1,0:T(8,128)(2,1)S(1)} copy(bf16[1,8,1024,128]{3,2,1,0:T(8,128)(2,1)} %param.7) | data formatting | bytes 4194304 | tf_op args[0]
  11.3 28.9 %all-gather.2.cloned.1.call-done = bf16[8,1024,128]{1,2,0:T(8,128)(2,1)} async-done(((bf16[8,128,128]{1,2,0:T(8,128)(2,1)}), bf16[8,1024,128]{1,2,0:T(8,128)(2,1)}) %all-gather.2.cloned.1.call-update) | async-done | bytes 2097168 | tf_op jit(solution)/shard_map/all_gather | solution.py:35
  40.2 1.6 %fusion.12 = f32[8,64,64]{1,2,0:T(8,128)S(1)} fusion(bf16[8,1024,128]{1,2,0:T(8,128)(2,1)} %all-gather.2.cloned.1.call-done, bf16[8,1024,128]{1,2,0:T(8,128)(2,1)S(1)} %bitcast.103), kind=kOutput, calls=%fused_computation.15 | convolution fusion | flops 67108864 | bytes 2228224 | tf_op jit(solution)/shard_map/kbr,kbs->krs/dot_general | solution.py:36
  41.8 2.3 %fusion.10 = f32[8,64,1024]{2,1,0:T(8,128)S(1)} fusion(f32[8,64,64]{1,2,0:T(8,128)S(1)} %fusion.12, bf16[8,1024,128]{1,2,0:T(8,128)(2,1)} %bitcast.104), kind=kOutput, calls=%fused_computation.13 | convolution fusion | flops 402653184 | bytes 3276800 | tf_op jit(solution)/shard_map/kbr,krs->kbs/dot_general | solution.py:41
  44.2 1.6 %fusion.18 = f32[8,64,64]{1,2,0:T(8,128)S(1)} fusion(bf16[8,1024,128]{1,2,0:T(8,128)(2,1)S(1)} %copy-done.2, f32[64,1024]{1,0:T(8,128)S(1)} %copy-done), kind=kOutput, calls=%fused_computation.25 | convolution fusion | flops 402653184 | bytes 1441792 | tf_op jit(solution)/shard_map/nbr,sb->nrs/dot_general | solution.py:13
  45.8 1.6 %fusion.6 = f32[1024,64]{0,1:T(8,128)S(1)} fusion(f32[8,64,64]{1,2,0:T(8,128)S(1)} %fusion.18, f32[8,64,1024]{2,1,0:T(8,128)S(1)} %fusion.10, f32[8]{0:T(128)S(1)} %convert_bitcast_fusion), kind=kOutput, calls=%fused_computation.6 | convolution fusion | flops 403177472 | bytes 2490400 | tf_op jit(solution)/shard_map/nbr,nrs->bs/dot_general | solution.py:14
  47.5 1.0 select_reduce_fusion.3
  49.1 0.1 copy.20
  49.2 5.8 %cholesky.59 = f32[64,64]{1,0:T(8,128)S(1)} custom-call(f32[64,64]{1,0:T(8,128)S(1)} %fusion.48), custom_call_target="Cholesky" | custom-call | tf_op jit(solution)/shard_map/jit(cholesky)/cholesky | solution.py:19
  55.1 0.6 compare_reduce_fusion.2
  55.7 0.7 fusion.37
  56.4 4.9 %custom-call.7 = f32[1,64,64]{1,2,0:T(8,128)S(1)} custom-call(f32[1,64,64]{2,1,0:T(8,128)S(1)} %fusion.37), custom_call_target="InvertDiagBlocksLowerTriangular" | custom-call | tf_op jit(solution)/shard_map/triangular_solve/custom-call.0 | solution.py:20
  61.3 0.0 copy-start.3
  61.3 0.4 fusion.46
  61.7 3.2 %fusion = f32[8,64,64]{1,2,0:T(8,128)S(1)} fusion(f32[8,64,1024]{2,1,0:T(8,128)S(1)} %fusion.10, f32[8]{0:T(128)S(1)} %convert_bitcast_fusion, f32[64,1024]{1,0:T(8,128)S(1)} %fusion.46), kind=kOutput, calls=%fused_computation | convolution fusion | flops 403177472 | bytes 2490400 | tf_op jit(solution)/shard_map/nbr,bs->nrs/dot_general | solution.py:21
  65.0 0.7 convolution_bitcast_fusion.4
  65.7 1.5 %collective-permute-start = (f32[1024,128]{0,1:T(8,128)S(1)}, f32[1024,128]{0,1:T(8,128)S(1)}, u32[]{:S(2)}, u32[]{:S(2)}) collective-permute-start(f32[1024,128]{0,1:T(8,128)S(1)} %pad_maximum_fusion.2), channel_id=1, source_target_pairs={{0,1},{1,0},{2,3},{3,2},{4,5},{5,4},{6,7},{7,6},{8,9},{9,8},{10,11... | collective-permute-start | bytes 1572872 | tf_op jit(solution)/shard_map/ppermute | solution.py:8
  67.3 12.6 %collective-permute-done = f32[1024,128]{0,1:T(8,128)S(1)} collective-permute-done((f32[1024,128]{0,1:T(8,128)S(1)}, f32[1024,128]{0,1:T(8,128)S(1)}, u32[]{:S(2)}, u32[]{:S(2)}) %collective-permute-start) | collective-permute-done | bytes 524320 | tf_op jit(solution)/shard_map/ppermute | solution.py:8
  79.9 0.1 select_bitcast_fusion.3
  80.0 0.9 fusion.29
  80.9 0.4 convolution_bitcast_fusion.3
  81.3 1.0 select_reduce_fusion.2
  82.9 0.1 copy.23
  83.0 5.8 %cholesky.70 = f32[64,64]{1,0:T(8,128)S(1)} custom-call(f32[64,64]{1,0:T(8,128)S(1)} %fusion.45), custom_call_target="Cholesky" | custom-call | tf_op jit(solution)/shard_map/jit(cholesky)/cholesky | solution.py:19
  88.9 0.6 compare_reduce_fusion.1
  89.6 0.7 fusion.38
  90.2 4.9 %custom-call.8 = f32[1,64,64]{1,2,0:T(8,128)S(1)} custom-call(f32[1,64,64]{2,1,0:T(8,128)S(1)} %fusion.38), custom_call_target="InvertDiagBlocksLowerTriangular" | custom-call | tf_op jit(solution)/shard_map/triangular_solve/custom-call.0 | solution.py:20
  95.1 0.6 fusion.43
  95.8 0.9 fusion.24
  96.7 0.4 convolution_bitcast_fusion.2
  97.1 2.5 %collective-permute-start.1 = (f32[1024,128]{0,1:T(8,128)S(1)}, f32[1024,128]{0,1:T(8,128)S(1)}, u32[]{:S(2)}, u32[]{:S(2)}) collective-permute-start(f32[1024,128]{0,1:T(8,128)S(1)} %pad_maximum_fusion.3), channel_id=1, source_target_pairs={{0,2},{1,3},{2,0},{3,1},{4,6},{5,7},{6,4},{7,5},{8,10},{9,11},{10,... | collective-permute-start | bytes 1572872 | tf_op jit(solution)/shard_map/ppermute | solution.py:8
  99.6 23.0 %collective-permute-done.1 = f32[1024,128]{0,1:T(8,128)S(1)} collective-permute-done((f32[1024,128]{0,1:T(8,128)S(1)}, f32[1024,128]{0,1:T(8,128)S(1)}, u32[]{:S(2)}, u32[]{:S(2)}) %collective-permute-start.1) | collective-permute-done | bytes 524320 | tf_op jit(solution)/shard_map/ppermute | solution.py:8
  122.6 0.1 select_bitcast_fusion.1
  122.7 0.9 fusion.27
  123.6 0.4 convolution_bitcast_fusion.1
  124.1 1.0 select_reduce_fusion.1
  125.7 0.1 copy.26
  125.8 5.8 %cholesky.81 = f32[64,64]{1,0:T(8,128)S(1)} custom-call(f32[64,64]{1,0:T(8,128)S(1)} %fusion.42), custom_call_target="Cholesky" | custom-call | tf_op jit(solution)/shard_map/jit(cholesky)/cholesky | solution.py:19
  131.7 0.6 compare_reduce_fusion
  132.3 0.7 fusion.39
  133.0 4.9 %custom-call.9 = f32[1,64,64]{1,2,0:T(8,128)S(1)} custom-call(f32[1,64,64]{2,1,0:T(8,128)S(1)} %fusion.39), custom_call_target="InvertDiagBlocksLowerTriangular" | custom-call | tf_op jit(solution)/shard_map/triangular_solve/custom-call.0 | solution.py:20
  137.9 0.4 bitcast_multiply_fusion
  138.3 0.9 fusion.22
  139.2 0.4 fusion.9
  139.7 0.8 copy.27
  (22 shorter events, 0.3 us)
Async XLA Ops:
  6.5 37.6 %copy-start = (f32[64,1024]{1,0:T(8,128)S(1)}, f32[64,1024]{1,0:T(8,128)}, u32[]{:S(2)}) copy-start(f32[64,1024]{1,0:T(8,128)} %param.10) | copy-start | bytes 786436
  6.5 33.6 %all-gather.2.cloned.1.call-start = ((), (), s32[]{:S(2)}) async-start(), calls=%async_computation | async-start | bytes 2359296 | tf_op jit(solution)/shard_map/all_gather | solution.py:35
  8.4 2.9 %copy-start.4 = (s32[1,8]{1,0:T(1,128)S(1)}, s32[1,8]{1,0:T(1,128)}, u32[]{:S(2)}) copy-start(s32[1,8]{1,0:T(1,128)} %param.9) | copy-start | bytes 100
  11.3 28.9 %copy-start.1 = (bf16[1,8,1024,128]{2,3,1,0:T(8,128)(2,1)}, bf16[1,8,1024,128]{2,3,1,0:T(8,128)(2,1)S(1)}, u32[]{:S(2)}) copy-start(bf16[1,8,1024,128]{2,3,1,0:T(8,128)(2,1)S(1)} %copy.16) | copy-start | bytes 6291460
  41.8 2.4 %copy-start.2 = (bf16[8,1024,128]{1,2,0:T(8,128)(2,1)S(1)}, bf16[8,1024,128]{1,2,0:T(8,128)(2,1)}, u32[]{:S(2)}) copy-start(bf16[8,1024,128]{1,2,0:T(8,128)(2,1)} %all-gather.2.cloned.1.call-done) | copy-start | bytes 6291460
  61.3 3.7 %copy-start.3 = (bf16[8,1024,128]{1,2,0:T(8,128)(2,1)S(1)}, bf16[8,1024,128]{1,2,0:T(8,128)(2,1)}, u32[]{:S(2)}) copy-start(bf16[8,1024,128]{1,2,0:T(8,128)(2,1)} %all-gather.2.cloned.1.call-done) | copy-start | bytes 6291460
  65.7 14.1 %collective-permute-start = (f32[1024,128]{0,1:T(8,128)S(1)}, f32[1024,128]{0,1:T(8,128)S(1)}, u32[]{:S(2)}, u32[]{:S(2)}) collective-permute-start(f32[1024,128]{0,1:T(8,128)S(1)} %pad_maximum_fusion.2), channel_id=1, source_target_pairs={{0,1},{1,0},{2,3},{3,2},{4,5},{5,4},{6,7},{7,6},{8,9},{9,8},{10,11... | collective-permute-start | bytes 1572872 | tf_op jit(solution)/shard_map/ppermute | solution.py:8
  97.1 25.5 %collective-permute-start.1 = (f32[1024,128]{0,1:T(8,128)S(1)}, f32[1024,128]{0,1:T(8,128)S(1)}, u32[]{:S(2)}, u32[]{:S(2)}) collective-permute-start(f32[1024,128]{0,1:T(8,128)S(1)} %pad_maximum_fusion.3), channel_id=1, source_target_pairs={{0,2},{1,3},{2,0},{3,1},{4,6},{5,7},{6,4},{7,5},{8,10},{9,11},{10,... | collective-permute-start | bytes 1572872 | tf_op jit(solution)/shard_map/ppermute | solution.py:8
Sparse Core Ops, SparseCore 0:
  9.2 30.8 all-gather.1
where the time goes:
time: 148 us; the launch traced here: 147 us
  waiting for transfers between devices  64.5 us (44%)
  other arithmetic  36.6 us (25%)
  matrix products  20.8 us (14%)
  between operations  15.7 us (11%)
  local copies, waits for them, and re-layouts  5.69 us (4%)
  starting transfers between devices  4.01 us (3%)
    ppermute x2, waiting for transfers between devices, from_partner(): lax.ppermute(shard, axis, [(i, i ^ 1 << stride) for i in range(lax.axis_s...  35.6 us
    all_gather x1, waiting for transfers between devices, body(): panel = lax.all_gather(panel_factors, 'rows', axis=1, tiled=True)  28.9 us
    another operation x9, other arithmetic, compress(): chol = jnp.linalg.cholesky(gram)  19.6 us
    another operation x6, other arithmetic, compress(): lax.linalg.triangular_solve(chol, span, left_side=False, lower=True, tran...  16.6 us
    dot_general x3, matrix products, compress(): coef = jnp.einsum('nbr,bs->nrs', lefts, basis, precision=hi)  4.99 us
    unnamed x12, local copies, waits for them, and re-layouts  4.71 us
    ppermute x2, starting transfers between devices, from_partner(): lax.ppermute(shard, axis, [(i, i ^ 1 << stride) for i in range(lax.axis_s...  4.01 us
    dot_general x3, matrix products, compress(): proj = jnp.einsum('nbr,sb->nrs', rights, sketch, precision=hi)  3.37 us
  transfers between devices with their start and end apart: 3, of which 3 were waited for; matrix products, arithmetic and copies ran while one was open for 2% of the time, Pallas kernels for 0%

commit v1 on v0

v1 whole, which is shorter than its diff:
```python
import functools

import jax
import jax.numpy as jnp
from jax import lax
from jax.experimental import pallas as pl
from jax.experimental.pallas import tpu as pltpu
from jax.sharding import PartitionSpec as P

HI = lax.Precision.HIGHEST
F32 = jnp.float32
BF16 = jnp.bfloat16
MESH = pl.DeviceIdType.MESH
NN = (((1,), (0,)), ((), ()))
NT = (((1,), (1,)), ((), ()))
TN = (((0,), (0,)), ((), ()))


def dot(a, b, dims):
    return lax.dot_general(a, b, dims, precision=HI, preferred_element_type=F32)


def dot16(a, b, dims):
    return lax.dot_general(a, b, dims, preferred_element_type=F32)


def split3(x):
    hi = x.astype(BF16)
    rest = x - hi.astype(F32)
    mid = rest.astype(BF16)
    low = (rest - mid.astype(F32)).astype(BF16)
    return jnp.concatenate([hi, mid, low], axis=0)


def sum3(x, rank):
    return x[:rank] + (x[rank : 2 * rank] + x[2 * rank :])


def iotas(rank):
    shape = (rank, 2 * rank)
    return lax.broadcasted_iota(jnp.int32, shape, 0), lax.broadcasted_iota(jnp.int32, shape, 1)


def inverse_factor(gram, rank):
    row, col = iotas(rank)
    diag = col == row + rank
    trace = jnp.sum(jnp.where(diag, gram, 0.0), keepdims=True)
    shift = 0.001 * trace / rank + 1e-20
    m = gram + jnp.where(diag, shift, 0.0) + jnp.where(col == row, 1.0, 0.0)
    for j in range(rank - 1):
        start = (j + 1) // 8 * 8
        pivot_row = m[j : j + 1, :]
        scaled = pivot_row / m[j : j + 1, rank + j : rank + j + 1]
        tail = m[start:]
        factor = tail[:, rank + j : rank + j + 1]
        if (j + 1) % 8:
            factor = jnp.where(row[start:, :1] > j, factor, 0.0)
        tail = tail - factor * scaled
        m = jnp.concatenate([m[:start], tail], axis=0) if start else tail
    pivots = jnp.sum(jnp.where(diag, m, 0.0), axis=1, keepdims=True)
    return (m * lax.rsqrt(pivots))[:, :rank]


def below(x):
    return jnp.concatenate([jnp.zeros_like(x), x], axis=0)


def above(x):
    return jnp.concatenate([x, jnp.zeros_like(x)], axis=0)


def kernel(rows, upd, tile_ref, panel_ref, nonnull_ref, sketch_ref, out_ref,
           panel, inner, proj, *rest):
    levels = upd.bit_length() - 1
    stages, pairs, apairs, ebufs = (rest[v * levels : (v + 1) * levels] for v in range(4))
    chip_send, chip_recv, sib_send, sib_recv, wz_sem, a_sem, e_send, e_recv = rest[4 * levels :]
    count, block, width = panel_ref.shape
    order = tile_ref.shape[2]
    rank = width // 2
    me, z = lax.axis_index("rows"), lax.axis_index("upd")
    chips = rows // 2
    chip, core = me // 2, lax.rem(me, 2)
    sibling = 2 * chip + 1 - core

    def chip_at(offset):
        return lax.rem(chip + offset + chips, chips)

    barrier = pltpu.get_barrier_semaphore()
    peers = [(sibling, z)] + [(2 * chip_at(c) + core, z) for c in range(1, chips)]
    peers += [(me, lax.rem(z + t, upd)) for t in range(1, upd)]
    for peer in peers:
        pl.semaphore_signal(barrier, inc=1, device_id=peer, device_id_type=MESH)
    pl.semaphore_wait(barrier, len(peers))

    def slot(index):
        return panel.at[:, pl.ds(pl.multiple_of(index * block, block), block), :]

    def chip_copy(offset, src, owner):
        return pltpu.make_async_remote_copy(
            src_ref=src, dst_ref=slot(owner), send_sem=chip_send.at[offset],
            recv_sem=chip_recv.at[offset], device_id=(2 * chip_at(offset) + core, z),
            device_id_type=MESH)

    def sib_copy(offset, src, owner):
        return pltpu.make_async_remote_copy(
            src_ref=src, dst_ref=slot(owner), send_sem=sib_send.at[offset],
            recv_sem=sib_recv.at[offset], device_id=(sibling, z), device_id_type=MESH)

    sends = []
    for c in range(1, chips):
        copy = chip_copy(c, panel_ref, me)
        copy.start()
        sends.append(copy)
    copy = sib_copy(0, panel_ref, me)
    copy.start()
    sends.append(copy)
    panel[:, pl.ds(pl.multiple_of(me * block, block), block), :] = panel_ref[...]
    sketch3 = split3(sketch_ref[...])
    for c in range(1, chips):
        source = 2 * chip_at(-c) + core
        chip_copy(c, slot(source), source).wait_recv()
        copy = sib_copy(c, slot(source), source)
        copy.start()
        sends.append(copy)
    for c in range(chips):
        source = 2 * chip_at(-c) + 1 - core
        sib_copy(c, slot(source), source).wait_recv()
    for copy in sends:
        copy.wait_send()

    row, col = iotas(rank)
    left = col < rank
    corner = below(jnp.where(left, 0.0, 1.0))
    span = jnp.zeros((3 * rank, order), F32)
    for k in range(count):
        weight = nonnull_ref[0, k].astype(F32)
        mid = dot16(tile_ref[0, k], panel[k], TN) * (corner * weight)
        inner[k] = mid
        pk = sum3(dot16(sketch3, panel[k], NN), rank)
        proj[k] = pk
        t = pltpu.roll(dot(pltpu.roll(pk, rank, 1), mid, NT), rank, 1)
        span += dot16(split3(t), tile_ref[0, k], NT)
    span = sum3(span, rank)
    linv = inverse_factor(dot(span, below(span), NT), rank)
    basis = dot(linv, span, NN)
    basis3 = split3(basis)
    image = jnp.zeros((3 * rank, order), F32)
    a_own = jnp.zeros((rank, width), F32)
    for k in range(count):
        wu = pltpu.roll(sum3(dot16(basis3, tile_ref[0, k], NN), rank), rank, 1)
        coef = pltpu.roll(dot(wu, inner[k], NN), rank, 1)
        a_own += dot(proj[k], above(coef), NT)
        image += dot16(split3(coef), panel[k], NT)
    image = sum3(image, rank)
    packed = jnp.concatenate([basis, image], axis=0).T
    stages[0][...] = packed.reshape(stages[0].shape)

    for level in range(levels):
        pair, apair, ebuf = pairs[level], apairs[level], ebufs[level]
        stage = stages[level]
        size = 2 << level
        bit = lax.rem(z // (1 << level), 2)
        partner = z + (1 - 2 * bit) * (1 << level)
        wz_copy = pltpu.make_async_remote_copy(
            src_ref=stage.at[:, 1 - bit], dst_ref=pair.at[bit], send_sem=wz_sem.at[level, 0],
            recv_sem=wz_sem.at[level, 1], device_id=(me, partner), device_id_type=MESH)
        wz_copy.start()
        apair[bit] = a_own
        a_copy = pltpu.make_async_remote_copy(
            src_ref=apair.at[bit], dst_ref=apair.at[bit], send_sem=a_sem.at[level, 0],
            recv_sem=a_sem.at[level, 1], device_id=(me, partner), device_id_type=MESH)
        a_copy.start()
        pair[bit] = stage[:, bit]
        a_copy.wait()
        wz_copy.wait()

        part = order // size
        low, high = pair[0].reshape(part, width), pair[1].reshape(part, width)
        a_low, a_high = apair[0], apair[1]
        span = dot(low, a_low, NT) + dot(high, a_high, NT)
        cross_low, cross_high = dot(span, low, TN), dot(span, high, TN)
        place = lax.rem(z, size)
        ebuf[place] = jnp.where(left, cross_low, pltpu.roll(cross_high, rank, 1))
        copies = []
        for t in range(1, size):
            other = z - place + lax.rem(place + t, size)
            copy = pltpu.make_async_remote_copy(
                src_ref=ebuf.at[place], dst_ref=ebuf.at[place], send_sem=e_send.at[level, t],
                recv_sem=e_recv.at[level, t], device_id=(me, other), device_id_type=MESH)
            copy.start()
            copies.append(copy)
        for copy in copies:
            copy.wait()
        cross = ebuf[0]
        for t in range(1, size):
            cross += ebuf[t]
        a_both = a_low + pltpu.roll(a_high, rank, 1)
        linv = inverse_factor(dot(cross, below(a_both), NT), rank)
        coef = dot(linv, cross, NN)
        a_own = dot(a_both, above(coef), NT)
        coef_low = pltpu.roll(jnp.where(left, coef, 0.0), rank, 1)
        coef_high = jnp.where(left, 0.0, coef)
        packed = (dot(span, above(linv), NT) + dot(low, below(coef_low), NT)
                  + dot(high, below(coef_high), NT))
        if level + 1 < levels:
            stages[level + 1][...] = packed.reshape(stages[level + 1].shape)
    scale = jnp.sqrt(F32(order))
    first = lax.broadcasted_iota(jnp.int32, packed.shape, 1) < rank
    out_ref[0] = packed * jnp.where(first, scale, 1.0 / scale)


def solution(mesh):
    rows, upd = mesh.shape["rows"], mesh.shape["upd"]
    levels = upd.bit_length() - 1
    in_specs = (P("rows", "upd", None, None), P("upd", "rows", None), P("rows", "upd"), P())
    out_specs = P("rows", "upd", None)

    def body(tiles, panel, nonnull, sketch):
        count, block, width = panel.shape
        order = tiles.shape[2]
        rank = width // 2
        share = order // upd
        dma = pltpu.SemaphoreType.DMA
        scratch = [
            pltpu.VMEM((count, order, width), BF16),
            pltpu.VMEM((count, width, width), F32),
            pltpu.VMEM((count, rank, width), F32),
        ]
        scratch += [pltpu.VMEM((upd >> v + 1, 2, share, width), F32) for v in range(levels)]
        scratch += [pltpu.VMEM((2, upd >> v + 1, share, width), F32) for v in range(levels)]
        scratch += [pltpu.VMEM((2, rank, width), F32) for v in range(levels)]
        scratch += [pltpu.VMEM((2 << v, rank, width), F32) for v in range(levels)]
        scratch += [dma((rows // 2,))] * 4 + [dma((levels, 2))] * 2 + [dma((levels, upd))] * 2
        vmem = pl.BlockSpec(memory_space=pltpu.VMEM)
        return pl.pallas_call(
            functools.partial(kernel, rows, upd),
            out_shape=jax.ShapeDtypeStruct((1, share, width), F32),
            in_specs=[vmem, vmem, pl.BlockSpec(memory_space=pltpu.SMEM), vmem],
            out_specs=vmem,
            scratch_shapes=scratch,
            compiler_params=pltpu.CompilerParams(
                collective_id=0, has_side_effects=True, vmem_limit_bytes=48 * 1024 * 1024),
        )(tiles, panel, nonnull, sketch)

    return jax.shard_map(body, mesh=mesh, in_specs=in_specs, out_specs=out_specs, check_vma=False)
```

time: 148 us -> 84.4 us (0.57)
  Pallas kernels: 0 us -> 79.4 us
  waiting for transfers between devices: 64.5 us -> 0 us
  other arithmetic: 36.6 us -> 0 us
  matrix products: 20.8 us -> 0 us
  between operations: 15.7 us -> 0.01 us
  starting transfers between devices: 4.01 us -> 0 us
    pallas_call x0 -> x1, Pallas kernels: none -> 79.4 us  [body(): pl.pallas_call(functools.partial(kernel, rows, upd), out_shape=jax.ShapeD...]
    another operation x17 -> x0, other arithmetic: 36.4 us -> none  [the longest x9 19.6 us: compress(): chol = jnp.linalg.cholesky(gram)]
    ppermute x2 -> x0, waiting for transfers between devices: 35.6 us -> none  [from_partner(): lax.ppermute(shard, axis, [(i, i ^ 1 << stride) for i in range(lax.axis_s...]
    all_gather x1 -> x0, waiting for transfers between devices: 28.9 us -> none  [body(): panel = lax.all_gather(panel_factors, 'rows', axis=1, tiled=True)]
    dot_general x17 -> x0, matrix products: 19.4 us -> none  [the longest x3 4.99 us: compress(): coef = jnp.einsum('nbr,bs->nrs', lefts, basis, precision=hi)]
    ppermute x2 -> x0, starting transfers between devices: 4.01 us -> none  [from_partner(): lax.ppermute(shard, axis, [(i, i ^ 1 << stride) for i in range(lax.axis_s...]
    unnamed x12 -> x9, local copies, waits for them, and re-layouts: 4.71 us -> 4.8 us
  transfers between devices with their start and end apart: 3 -> 0, of which waited for: 3 -> 0; matrix products, arithmetic and copies ran while one was open for 2% -> 0% of each run, Pallas kernels for 0% -> 0%
where the time goes in v1:
time: 84.4 us; the launch traced here: 84.2 us
  Pallas kernels  79.4 us (94%)
  local copies, waits for them, and re-layouts  4.8 us (6%)
    pallas_call x1, Pallas kernels, body(): pl.pallas_call(functools.partial(kernel, rows, upd), out_shape=jax.ShapeD...  79.4 us
    unnamed x9, local copies, waits for them, and re-layouts  4.8 us

profile of v1, /device:TPU:0, one launch (start us, length us, event | category | flops | bytes accessed | tf_op | source)
XLA Modules:
  0.0 84.2 jit_solution(9983684096251561962)
XLA Ops:
  0.0 0.0 copy-start
  0.0 1.6 %copy-done = bf16[1,8,1024,128]{3,2,1,0:T(8,128)(2,1)S(1)} copy-done((bf16[1,8,1024,128]{3,2,1,0:T(8,128)(2,1)S(1)}, bf16[1,8,1024,128]{3,2,1,0:T(8,128)(2,1)}, u32[]{:S(2)}) %copy-start) | copy-done | bytes 2097176
  1.6 0.0 copy-start.1
  1.6 0.9 %copy-done.1 = bf16[8,128,128]{2,1,0:T(8,128)(2,1)S(1)} copy-done((bf16[8,128,128]{2,1,0:T(8,128)(2,1)S(1)}, bf16[8,128,128]{2,1,0:T(8,128)(2,1)}, u32[]{:S(2)}) %copy-start.1) | copy-done | bytes 262168
  2.5 0.0 copy-start.2
  2.5 0.9 %copy-done.2 = f32[64,1024]{1,0:T(8,128)S(1)} copy-done((f32[64,1024]{1,0:T(8,128)S(1)}, f32[64,1024]{1,0:T(8,128)}, u32[]{:S(2)}) %copy-start.2) | copy-done | bytes 262168
  3.5 0.0 copy-start.3
  3.5 0.7 copy-done.3
  4.1 79.4 %shard_map.46 = f32[1,256,128]{2,1,0:T(8,128)S(1)} custom-call(bf16[1,8,1024,128]{3,2,1,0:T(8,128)(2,1)S(1)} %copy-done, bf16[8,128,128]{2,1,0:T(8,128)(2,1)S(1)} %copy-done.1, s32[1,8]{1,0:T(1,128)S(1)} %copy-done.3, f32[64,1024]{1,0:T(8,128)S(1)} %copy-done.2), custom_call_target="tpu_custom_call" | custom-call | tf_op jit(solution)/shard_map/pallas_call | solution.py:235
  83.6 0.7 copy.6
Async XLA Ops:
  0.0 1.6 %copy-start = (bf16[1,8,1024,128]{3,2,1,0:T(8,128)(2,1)S(1)}, bf16[1,8,1024,128]{3,2,1,0:T(8,128)(2,1)}, u32[]{:S(2)}) copy-start(bf16[1,8,1024,128]{3,2,1,0:T(8,128)(2,1)} %tile_ref.1) | copy-start | bytes 6291460
  1.6 0.9 %copy-start.1 = (bf16[8,128,128]{2,1,0:T(8,128)(2,1)S(1)}, bf16[8,128,128]{2,1,0:T(8,128)(2,1)}, u32[]{:S(2)}) copy-start(bf16[8,128,128]{2,1,0:T(8,128)(2,1)} %panel_ref.1) | copy-start | bytes 786436
  2.5 0.9 %copy-start.2 = (f32[64,1024]{1,0:T(8,128)S(1)}, f32[64,1024]{1,0:T(8,128)}, u32[]{:S(2)}) copy-start(f32[64,1024]{1,0:T(8,128)} %sketch_ref.1) | copy-start | bytes 786436
  3.5 0.7 copy-start.3

commit v2 on v1

v2 whole, which is shorter than its diff:
```python
import functools

import jax
import jax.numpy as jnp
from jax import lax
from jax.experimental import pallas as pl
from jax.experimental.pallas import tpu as pltpu
from jax.sharding import PartitionSpec as P

HI = lax.Precision.HIGHEST
GROUP = 4
PARTS = 4
F32 = jnp.float32
BF16 = jnp.bfloat16
MESH = pl.DeviceIdType.MESH
NN = (((1,), (0,)), ((), ()))
NT = (((1,), (1,)), ((), ()))
TN = (((0,), (0,)), ((), ()))


def dot(a, b, dims):
    return lax.dot_general(a, b, dims, precision=HI, preferred_element_type=F32)


def dot16(a, b, dims):
    return lax.dot_general(a, b, dims, preferred_element_type=F32)


def split3(x):
    hi = x.astype(BF16)
    rest = x - hi.astype(F32)
    mid = rest.astype(BF16)
    low = (rest - mid.astype(F32)).astype(BF16)
    return jnp.concatenate([hi, mid, low], axis=0)


def sum3(x, rank):
    return x[:rank] + (x[rank : 2 * rank] + x[2 * rank :])


def iotas(rank):
    shape = (rank, 2 * rank)
    return lax.broadcasted_iota(jnp.int32, shape, 0), lax.broadcasted_iota(jnp.int32, shape, 1)


def inverse_factor(gram, rank):
    row, col = iotas(rank)
    diag = col == row + rank
    trace = jnp.sum(jnp.where(diag, gram, 0.0), keepdims=True)
    shift = 0.001 * trace / rank + 1e-20
    m = gram + jnp.where(diag, shift, 0.0) + jnp.where(col == row, 1.0, 0.0)
    for base in range(0, rank, GROUP):
        start = base // 8 * 8
        tail = m[start:]
        shape = tail.shape
        columns = [
            jnp.broadcast_to(tail[:, rank + j : rank + j + 1], shape)
            for j in range(base, base + GROUP)
        ]
        below_row = row[start:]
        for step in range(GROUP):
            j = base + step
            at = j - start
            column = columns[step]
            factor = jnp.where(below_row > j, column * (1.0 / column[at : at + 1]), 0.0)
            for later in range(step + 1, GROUP):
                columns[later] = columns[later] - factor * columns[later][at : at + 1]
            tail = tail - factor * tail[at : at + 1]
        m = jnp.concatenate([m[:start], tail], axis=0) if start else tail
    pivots = jnp.sum(jnp.where(diag, m, 0.0), axis=1, keepdims=True)
    return (m * lax.rsqrt(pivots))[:, :rank]


def below(x):
    return jnp.concatenate([jnp.zeros_like(x), x], axis=0)


def above(x):
    return jnp.concatenate([x, jnp.zeros_like(x)], axis=0)


def twice(x, rank):
    return jnp.concatenate([x, pltpu.roll(x, rank, 1)], axis=0)


def kernel(rows, upd, tile_hbm, panel_hbm, nonnull_ref, sketch_hbm, out_ref,
           tile, panel, sketch, inner, proj, *rest):
    levels = upd.bit_length() - 1
    stages, zstages, pairs, zpairs, apairs, ebufs = (
        rest[v * levels : (v + 1) * levels] for v in range(6))
    (tile_sem, own_sem, sketch_sem, chip_send, chip_recv, sib_send, sib_recv,
     w_sem, z_sem, a_sem, e_send, e_recv) = rest[6 * levels :]
    count, block, width = panel_hbm.shape
    order = tile_hbm.shape[2]
    rank = width // 2
    step = count // PARTS
    me, z = lax.axis_index("rows"), lax.axis_index("upd")
    chips = rows // 2
    chip, core = me // 2, lax.rem(me, 2)
    sibling = 2 * chip + 1 - core

    sketch_copy = pltpu.make_async_copy(sketch_hbm, sketch, sketch_sem)
    sketch_copy.start()
    tile_copies, own_copies = [], []
    for g in range(PARTS):
        part = pl.ds(g * step, step)
        tile_copies.append(
            pltpu.make_async_copy(tile_hbm.at[0, part], tile.at[part], tile_sem.at[g]))
        tile_copies[g].start()

    def chip_at(offset):
        return lax.rem(chip + offset + chips, chips)

    barrier = pltpu.get_barrier_semaphore()
    peers = [(sibling, z)] + [(2 * chip_at(c) + core, z) for c in range(1, chips)]
    peers += [(me, lax.rem(z + t, upd)) for t in range(1, upd)]
    for peer in peers:
        pl.semaphore_signal(barrier, inc=1, device_id=peer, device_id_type=MESH)
    pl.semaphore_wait(barrier, len(peers))

    def slot(g, index):
        start = pl.multiple_of(index * block, block)
        return panel.at[pl.ds(g * step, step), pl.ds(start, block), :]

    def chip_copy(g, offset, src, owner):
        return pltpu.make_async_remote_copy(
            src_ref=src, dst_ref=slot(g, owner), send_sem=chip_send.at[g, offset],
            recv_sem=chip_recv.at[g, offset], device_id=(2 * chip_at(offset) + core, z),
            device_id_type=MESH)

    def sib_copy(g, offset, src, owner):
        return pltpu.make_async_remote_copy(
            src_ref=src, dst_ref=slot(g, owner), send_sem=sib_send.at[g, offset],
            recv_sem=sib_recv.at[g, offset], device_id=(sibling, z), device_id_type=MESH)

    sends = []
    for g in range(PARTS):
        own = panel_hbm.at[pl.ds(g * step, step)]
        copies = [chip_copy(g, c, own, me) for c in range(1, chips)] + [sib_copy(g, 0, own, me)]
        for copy in copies:
            copy.start()
        sends += copies
        own_copies.append(pltpu.make_async_copy(own, slot(g, me), own_sem.at[g]))
        own_copies[g].start()

    row, col = iotas(rank)
    left = col < rank
    corner = below(jnp.where(left, 0.0, 1.0))
    sketch_copy.wait()
    sketch3 = split3(sketch[...])
    span = jnp.zeros((3 * rank, order), F32)
    for g in range(PARTS):
        for c in range(1, chips):
            source = 2 * chip_at(-c) + core
            chip_copy(g, c, slot(g, source), source).wait_recv()
            copy = sib_copy(g, c, slot(g, source), source)
            copy.start()
            sends.append(copy)
        tile_copies[g].wait()
        own_copies[g].wait()
        for c in range(chips):
            source = 2 * chip_at(-c) + 1 - core
            sib_copy(g, c, slot(g, source), source).wait_recv()
        for k in range(g * step, (g + 1) * step):
            weight = nonnull_ref[0, k].astype(F32)
            mid = dot16(tile[k], panel[k], TN) * (corner * weight)
            inner[k] = mid
            pk = sum3(dot16(sketch3, panel[k], NN), rank)
            proj[k] = pk
            t = pltpu.roll(dot(pltpu.roll(pk, rank, 1), mid, NT), rank, 1)
            span += dot16(split3(t), tile[k], NT)
    span = sum3(span, rank)
    linv = inverse_factor(dot(span, below(span), NT), rank)
    basis = dot(linv, span, NN)

    def fold(x):
        cut = above(x).T.reshape(upd, 2, order // upd // 2, width)
        return cut[:, 0] + pltpu.roll(cut[:, 1], rank, 2)

    def exchange(level, src, dst, sem):
        bit = lax.rem(z // (1 << level), 2)
        partner = z + (1 - 2 * bit) * (1 << level)
        return pltpu.make_async_remote_copy(
            src_ref=src, dst_ref=dst, send_sem=sem.at[level, 0],
            recv_sem=sem.at[level, 1], device_id=(me, partner), device_id_type=MESH)

    def bit_of(level):
        return lax.rem(z // (1 << level), 2)

    def send_half(level, value, stage, pair, sem):
        bit = bit_of(level)
        stage[...] = value.reshape(stage.shape)
        copy = exchange(level, stage.at[:, 1 - bit], pair.at[bit], sem)
        copy.start()
        pair[bit] = stage[:, bit]
        return copy

    def send_sketch(level, value):
        bit = bit_of(level)
        apairs[level][bit] = value
        copy = exchange(level, apairs[level].at[bit], apairs[level].at[bit], a_sem)
        copy.start()
        return copy

    w_copy = send_half(0, fold(basis), stages[0], pairs[0], w_sem)
    basis3 = split3(basis)
    a_own = jnp.zeros((rank, width), F32)
    coefs = []
    for k in range(count):
        wu = pltpu.roll(sum3(dot16(basis3, tile[k], NN), rank), rank, 1)
        coef = pltpu.roll(dot(wu, inner[k], NN), rank, 1)
        a_own += dot(proj[k], above(coef), NT)
        inner[k, :rank] = coef
    a_copy = send_sketch(0, a_own)
    image = jnp.zeros((3 * rank, order), F32)
    for k in range(count):
        image += dot16(split3(inner[k, :rank]), panel[k], NT)
    z_copy = send_half(0, fold(sum3(image, rank)), zstages[0], zpairs[0], z_sem)

    for level in range(levels):
        pair, zpair, ebuf = pairs[level], zpairs[level], ebufs[level]
        size = 2 << level
        a_copy.wait()
        w_copy.wait()
        part = order // size // 2
        low, high = pair[0].reshape(part, width), pair[1].reshape(part, width)
        a_low, a_high = apairs[level][0], apairs[level][1]
        span = dot(low, twice(a_low, rank), NT) + dot(high, twice(a_high, rank), NT)
        cross_low, cross_high = dot(span, low, TN), dot(span, high, TN)
        cross_low = cross_low[:rank] + pltpu.roll(cross_low[rank:], rank, 1)
        cross_high = pltpu.roll(cross_high[:rank], rank, 1) + cross_high[rank:]
        place = lax.rem(z, size)
        ebuf[place] = jnp.where(left, cross_low, cross_high)
        copies = []
        for t in range(1, size):
            other = z - place + lax.rem(place + t, size)
            copy = pltpu.make_async_remote_copy(
                src_ref=ebuf.at[place], dst_ref=ebuf.at[place], send_sem=e_send.at[level, t],
                recv_sem=e_recv.at[level, t], device_id=(me, other), device_id_type=MESH)
            copy.start()
            copies.append(copy)
        for copy in copies:
            copy.wait()
        cross = ebuf[0]
        for t in range(1, size):
            cross += ebuf[t]
        a_both = a_low + pltpu.roll(a_high, rank, 1)
        linv = inverse_factor(dot(cross, below(a_both), NT), rank)
        wide = jnp.concatenate([linv, jnp.zeros_like(linv)], axis=1)
        basis = dot(span, twice(wide, rank), NT)
        coef = dot(linv, cross, NN)
        a_own = dot(a_both, above(coef), NT)
        if level + 1 < levels:
            w_copy = send_half(level + 1, basis, stages[level + 1], pairs[level + 1], w_sem)
            a_copy = send_sketch(level + 1, a_own)
        coef_low = jnp.where(left, coef, 0.0)
        coef_high = pltpu.roll(jnp.where(left, 0.0, coef), rank, 1)
        z_copy.wait()
        image = (dot(zpair[0].reshape(part, width), twice(coef_low, rank), NT)
                 + dot(zpair[1].reshape(part, width), twice(coef_high, rank), NT))
        if level + 1 < levels:
            z_copy = send_half(level + 1, image, zstages[level + 1], zpairs[level + 1], z_sem)
    first = lax.broadcasted_iota(jnp.int32, basis.shape, 1) < rank
    scale = jnp.sqrt(F32(order))
    basis, image = basis * scale, image / scale
    half = basis.shape[0]
    out_ref[0, :half] = jnp.where(first, basis, pltpu.roll(image, rank, 1))
    out_ref[0, half:] = jnp.where(first, pltpu.roll(basis, rank, 1), image)
    for copy in sends:
        copy.wait_send()


def solution(mesh):
    rows, upd = mesh.shape["rows"], mesh.shape["upd"]
    levels = upd.bit_length() - 1
    in_specs = (P("rows", "upd", None, None), P("upd", "rows", None), P("rows", "upd"), P())
    out_specs = P("rows", "upd", None)

    def body(tiles, panel, nonnull, sketch):
        count, block, width = panel.shape
        order = tiles.shape[2]
        rank = width // 2
        share = order // upd
        dma = pltpu.SemaphoreType.DMA
        scratch = [
            pltpu.VMEM((count, order, width), BF16),
            pltpu.VMEM((count, order, width), BF16),
            pltpu.VMEM((rank, order), F32),
            pltpu.VMEM((count, width, width), F32),
            pltpu.VMEM((count, rank, width), F32),
        ]
        scratch += [pltpu.VMEM((upd >> v + 1, 2, share // 2, width), F32) for v in range(levels)] * 2
        scratch += [pltpu.VMEM((2, upd >> v + 1, share // 2, width), F32) for v in range(levels)] * 2
        scratch += [pltpu.VMEM((2, rank, width), F32) for v in range(levels)]
        scratch += [pltpu.VMEM((2 << v, rank, width), F32) for v in range(levels)]
        scratch += [dma((PARTS,)), dma((PARTS,)), dma] + [dma((PARTS, rows // 2))] * 4
        scratch += [dma((levels, 2))] * 3 + [dma((levels, upd))] * 2
        hbm = pl.BlockSpec(memory_space=pl.ANY)
        vmem = pl.BlockSpec(memory_space=pltpu.VMEM)
        return pl.pallas_call(
            functools.partial(kernel, rows, upd),
            out_shape=jax.ShapeDtypeStruct((1, share, width), F32),
            in_specs=[hbm, hbm, pl.BlockSpec(memory_space=pltpu.SMEM), hbm],
            out_specs=vmem,
            scratch_shapes=scratch,
            compiler_params=pltpu.CompilerParams(
                collective_id=0, has_side_effects=True, vmem_limit_bytes=48 * 1024 * 1024),
        )(tiles, panel, nonnull, sketch)

    return jax.shard_map(body, mesh=mesh, in_specs=in_specs, out_specs=out_specs, check_vma=False)
```

time: 84.4 us -> 67.8 us (0.80)
  Pallas kernels: 79.4 us -> 62.8 us
    pallas_call x1, Pallas kernels: 79.4 us -> 62.8 us  [body(): pl.pallas_call(functools.partial(kernel, rows, upd), out_shape=jax.ShapeD...]
where the time goes in v2:
time: 67.8 us; the launch traced here: 67.6 us
  Pallas kernels  62.8 us (93%)
  local copies, waits for them, and re-layouts  4.8 us (7%)
    pallas_call x1, Pallas kernels, body(): pl.pallas_call(functools.partial(kernel, rows, upd), out_shape=jax.ShapeD...  62.8 us
    unnamed x9, local copies, waits for them, and re-layouts  4.8 us

profile of v2, /device:TPU:0, one launch (start us, length us, event | category | flops | bytes accessed | tf_op | source)
XLA Modules:
  0.0 67.6 jit_solution(1501069897796943965)
XLA Ops:
  0.0 0.0 copy-start
  0.0 1.6 %copy-done = bf16[1,8,1024,128]{3,2,1,0:T(8,128)(2,1)S(1)} copy-done((bf16[1,8,1024,128]{3,2,1,0:T(8,128)(2,1)S(1)}, bf16[1,8,1024,128]{3,2,1,0:T(8,128)(2,1)}, u32[]{:S(2)}) %copy-start) | copy-done | bytes 2097176
  1.6 0.0 copy-start.1
  1.6 0.9 %copy-done.1 = bf16[8,128,128]{2,1,0:T(8,128)(2,1)S(1)} copy-done((bf16[8,128,128]{2,1,0:T(8,128)(2,1)S(1)}, bf16[8,128,128]{2,1,0:T(8,128)(2,1)}, u32[]{:S(2)}) %copy-start.1) | copy-done | bytes 262168
  2.5 0.0 copy-start.2
  2.5 0.9 %copy-done.2 = f32[64,1024]{1,0:T(8,128)S(1)} copy-done((f32[64,1024]{1,0:T(8,128)S(1)}, f32[64,1024]{1,0:T(8,128)}, u32[]{:S(2)}) %copy-start.2) | copy-done | bytes 262168
  3.5 0.0 copy-start.3
  3.5 0.7 copy-done.3
  4.1 62.8 %shard_map.46 = f32[1,256,128]{2,1,0:T(8,128)S(1)} custom-call(bf16[1,8,1024,128]{3,2,1,0:T(8,128)(2,1)S(1)} %copy-done, bf16[8,128,128]{2,1,0:T(8,128)(2,1)S(1)} %copy-done.1, s32[1,8]{1,0:T(1,128)S(1)} %copy-done.3, f32[64,1024]{1,0:T(8,128)S(1)} %copy-done.2), custom_call_target="tpu_custom_call" | custom-call | tf_op jit(solution)/shard_map/pallas_call | solution.py:300
  66.9 0.7 copy.6
Async XLA Ops:
  0.0 1.6 %copy-start = (bf16[1,8,1024,128]{3,2,1,0:T(8,128)(2,1)S(1)}, bf16[1,8,1024,128]{3,2,1,0:T(8,128)(2,1)}, u32[]{:S(2)}) copy-start(bf16[1,8,1024,128]{3,2,1,0:T(8,128)(2,1)} %tile_hbm.1) | copy-start | bytes 6291460
  1.6 0.9 %copy-start.1 = (bf16[8,128,128]{2,1,0:T(8,128)(2,1)S(1)}, bf16[8,128,128]{2,1,0:T(8,128)(2,1)}, u32[]{:S(2)}) copy-start(bf16[8,128,128]{2,1,0:T(8,128)(2,1)} %panel_hbm.1) | copy-start | bytes 786436
  2.5 0.9 %copy-start.2 = (f32[64,1024]{1,0:T(8,128)S(1)}, f32[64,1024]{1,0:T(8,128)}, u32[]{:S(2)}) copy-start(f32[64,1024]{1,0:T(8,128)} %sketch_hbm.1) | copy-start | bytes 786436
  3.5 0.7 copy-start.3

commit v3 on v2

--- a/solution.py
+++ b/solution.py
@@ -8,8 +8,8 @@
 from jax.sharding import PartitionSpec as P
 
 HI = lax.Precision.HIGHEST
-GROUP = 4
-PARTS = 4
+GROUP = 16
+PARTS = 2
 F32 = jnp.float32
 BF16 = jnp.bfloat16
 MESH = pl.DeviceIdType.MESH

time: 67.8 us -> 63.2 us (0.932)
  Pallas kernels: 62.8 us -> 58.2 us
    pallas_call x1, Pallas kernels: 62.8 us -> 58.2 us  [body(): pl.pallas_call(functools.partial(kernel, rows, upd), out_shape=jax.ShapeD...]
where the time goes in v3:
time: 63.2 us; the launch traced here: 63 us
  Pallas kernels  58.2 us (92%)
  local copies, waits for them, and re-layouts  4.8 us (8%)
    pallas_call x1, Pallas kernels, body(): pl.pallas_call(functools.partial(kernel, rows, upd), out_shape=jax.ShapeD...  58.2 us
    unnamed x9, local copies, waits for them, and re-layouts  4.8 us

profile of v3, /device:TPU:0, one launch (start us, length us, event | category | flops | bytes accessed | tf_op | source)
XLA Modules:
  0.0 63.0 jit_solution(7876537042295260008)
XLA Ops:
  0.0 0.0 copy-start
  0.0 1.6 %copy-done = bf16[1,8,1024,128]{3,2,1,0:T(8,128)(2,1)S(1)} copy-done((bf16[1,8,1024,128]{3,2,1,0:T(8,128)(2,1)S(1)}, bf16[1,8,1024,128]{3,2,1,0:T(8,128)(2,1)}, u32[]{:S(2)}) %copy-start) | copy-done | bytes 2097176
  1.6 0.0 copy-start.1
  1.6 0.9 %copy-done.1 = bf16[8,128,128]{2,1,0:T(8,128)(2,1)S(1)} copy-done((bf16[8,128,128]{2,1,0:T(8,128)(2,1)S(1)}, bf16[8,128,128]{2,1,0:T(8,128)(2,1)}, u32[]{:S(2)}) %copy-start.1) | copy-done | bytes 262168
  2.5 0.0 copy-start.2
  2.5 0.9 %copy-done.2 = f32[64,1024]{1,0:T(8,128)S(1)} copy-done((f32[64,1024]{1,0:T(8,128)S(1)}, f32[64,1024]{1,0:T(8,128)}, u32[]{:S(2)}) %copy-start.2) | copy-done | bytes 262168
  3.5 0.0 copy-start.3
  3.5 0.7 %copy-done.3 = s32[1,8]{1,0:T(1,128)S(1)} copy-done((s32[1,8]{1,0:T(1,128)S(1)}, s32[1,8]{1,0:T(1,128)}, u32[]{:S(2)}) %copy-start.3) | copy-done | bytes 56
  4.1 58.2 %shard_map.46 = f32[1,256,128]{2,1,0:T(8,128)S(1)} custom-call(bf16[1,8,1024,128]{3,2,1,0:T(8,128)(2,1)S(1)} %copy-done, bf16[8,128,128]{2,1,0:T(8,128)(2,1)S(1)} %copy-done.1, s32[1,8]{1,0:T(1,128)S(1)} %copy-done.3, f32[64,1024]{1,0:T(8,128)S(1)} %copy-done.2), custom_call_target="tpu_custom_call" | custom-call | tf_op jit(solution)/shard_map/pallas_call | solution.py:300
  62.3 0.7 %copy.6 = f32[1,256,128]{2,1,0:T(8,128)} copy(f32[1,256,128]{2,1,0:T(8,128)S(1)} %shard_map.46) | data formatting | bytes 262144
Async XLA Ops:
  0.0 1.6 %copy-start = (bf16[1,8,1024,128]{3,2,1,0:T(8,128)(2,1)S(1)}, bf16[1,8,1024,128]{3,2,1,0:T(8,128)(2,1)}, u32[]{:S(2)}) copy-start(bf16[1,8,1024,128]{3,2,1,0:T(8,128)(2,1)} %tile_hbm.1) | copy-start | bytes 6291460
  1.6 0.9 %copy-start.1 = (bf16[8,128,128]{2,1,0:T(8,128)(2,1)S(1)}, bf16[8,128,128]{2,1,0:T(8,128)(2,1)}, u32[]{:S(2)}) copy-start(bf16[8,128,128]{2,1,0:T(8,128)(2,1)} %panel_hbm.1) | copy-start | bytes 786436
  2.5 0.9 %copy-start.2 = (f32[64,1024]{1,0:T(8,128)S(1)}, f32[64,1024]{1,0:T(8,128)}, u32[]{:S(2)}) copy-start(f32[64,1024]{1,0:T(8,128)} %sketch_hbm.1) | copy-start | bytes 786436
  3.5 0.7 %copy-start.3 = (s32[1,8]{1,0:T(1,128)S(1)}, s32[1,8]{1,0:T(1,128)}, u32[]{:S(2)}) copy-start(s32[1,8]{1,0:T(1,128)} %nonnull_ref.1) | copy-start | bytes 100
